TPU v7x, 256 devices: a whole 4x4x8 slice. The times are simulated.
256 devices in a mesh: depth: 16 (over x, z_lo), gx: 16 (over z_hi, y, core).
Axes of the slice: x: 4, y: 4, z: 8 (z_hi: 2, z_lo: 4; z = z_hi * 4 + z_lo), core: 2. Of those that a mesh axis runs over, the one named last changes fastest.
Arguments:
- volume: bfloat16 [64, 384, 2, 2048], P(None, 'depth', None, 'gx'), may hold values from -6 to 6
- conv_first: bfloat16 [3, 3, 3, 64, 64], replicated, may hold values from -0.15625 to 0.15625
- conv_second: bfloat16 [3, 3, 3, 64, 64], replicated, may hold values from -0.15625 to 0.15625
- mode_weights: bfloat16 [64, 64, 64], P('depth'), may hold values from -0.75 to 0.75
Outputs:
- next_volume: bfloat16 [64, 384, 2, 2048], P(None, 'depth', None, 'gx')
All inputs are finite; a program needn't handle non-finite values.
Results may differ from a plain program's by a relative error of at most 0.01.
Values may be sent and summed in bfloat16 or wider, within the bound.
A program may use at most 64 MiB of HBM per device.

v0:
```python
import math

import jax
import jax.numpy as jnp
from jax import lax
from jax.sharding import PartitionSpec as P

MODES = 32


def extended(cells, sides, width):
    for axis, dim in sides:
        count = lax.axis_size(axis)
        ends = count - 1
        head = lax.slice_in_dim(cells, 0, width, axis=dim)
        tail = lax.slice_in_dim(cells, cells.shape[dim] - width, cells.shape[dim], axis=dim)
        cells = jnp.concatenate(
            [
                lax.ppermute(tail, axis, [(i, (i + 1) % count) for i in range(ends)]),
                cells,
                lax.ppermute(head, axis, [((i + 1) % count, i) for i in range(ends)]),
            ],
            axis=dim,
        )
    return cells


def mode_basis(mode_index, depth_pos, total_z):
    frequency = jnp.where(mode_index < MODES, mode_index, mode_index - MODES + 1).astype(
        jnp.float32
    )
    odd_steps = (2 * depth_pos + 1).astype(jnp.float32)
    angles = frequency[:, None] * odd_steps[None, :] * (math.pi / (2.0 * total_z))
    values = jnp.where((mode_index < MODES)[:, None], jnp.cos(angles), jnp.sin(angles))
    return (values * math.sqrt(2.0 / total_z)).astype(jnp.bfloat16)


def convolve(padded, weights):
    padded = jnp.pad(padded, ((0, 0), (0, 0), (1, 1), (0, 0)))
    depth_cells = padded.shape[1] - 2
    row_cells = padded.shape[2] - 2
    col_cells = padded.shape[3] - 2
    summed = jnp.zeros((weights.shape[3], depth_cells, row_cells, col_cells), jnp.float32)
    for depth_tap in range(3):
        for row_tap in range(3):
            band = padded[:, depth_tap : depth_tap + depth_cells, row_tap : row_tap + row_cells, :]
            stacked = jnp.stack(
                [band[:, :, :, col_tap : col_tap + col_cells] for col_tap in range(3)], axis=0
            )
            summed = summed + jnp.einsum(
                "eoc,eczyx->ozyx",
                weights[depth_tap, row_tap],
                stacked,
                preferred_element_type=jnp.float32,
            )
    return summed


def local(volume, conv_first, conv_second, mode_weights):
    slab_depth = volume.shape[1]
    total_z = slab_depth * lax.axis_size("depth")
    depth_start = lax.axis_index("depth") * slab_depth
    depth_pos = depth_start + jnp.arange(slab_depth, dtype=jnp.int32)
    padded = extended(volume, (("depth", 1), ("gx", 3)), 1)
    hidden = jax.nn.gelu(convolve(padded, conv_first)).astype(jnp.bfloat16)
    padded_hidden = extended(hidden, (("depth", 1), ("gx", 3)), 1)
    local_part = convolve(padded_hidden, conv_second)
    mode_index = jnp.arange(lax.axis_size("depth") * mode_weights.shape[0], dtype=jnp.int32)
    summed = lax.psum_scatter(
        jnp.einsum(
            "mz,czyx->mcyx",
            mode_basis(mode_index, depth_pos, total_z),
            volume,
            preferred_element_type=jnp.float32,
        ).astype(jnp.bfloat16),
        "depth",
        scatter_dimension=0,
        tiled=True,
    )
    mixed = jnp.einsum(
        "moc,mcyx->moyx", mode_weights, summed, preferred_element_type=jnp.float32
    ).astype(jnp.bfloat16)
    block_modes = lax.all_gather(mixed, "depth", axis=0, tiled=True)
    mode_index = jnp.arange(block_modes.shape[0], dtype=jnp.int32)
    spectral = jnp.einsum(
        "mz,mcyx->czyx",
        mode_basis(mode_index, depth_pos, total_z),
        block_modes,
        preferred_element_type=jnp.float32,
    )
    return (volume.astype(jnp.float32) + local_part + spectral).astype(jnp.bfloat16)


def solution(mesh):
    placed = (P(None, "depth", None, "gx"), P(), P(), P("depth", None, None))
    return jax.shard_map(
        local, mesh=mesh, in_specs=placed, out_specs=P(None, "depth", None, "gx"), check_vma=False
    )
```

profile of v0, /device:TPU:16, one launch (start us, length us, event | category | flops | bytes accessed | tf_op | source)
XLA Modules:
  0.0 220.8 jit_solution(13006909521129716894)
XLA Ops:
  7.9 3.8 %collective-permute-start = (bf16[64,1,2,128]{3,0,2,1:T(8,128)(2,1)S(1)}, bf16[64,1,2,128]{3,0,2,1:T(8,128)(2,1)S(1)}, u32[]{:S(2)}, u32[]{:S(2)}) collective-permute-start(bf16[64,1,2,128]{3,0,2,1:T(8,128)(2,1)S(1)} %get-tuple-element.71), channel_id=1, source_target_pairs={{0,16},{16,32},{32,48},{48,64},{64,80},{80,96},{96,112},{112,128},... | collective-permute-start | bytes 98312 | tf_op jit(solution)/shard_map/ppermute | solution.py:19
  13.1 2.0 fusion.79
  15.1 2.7 %copy.208 = bf16[64,64,2,128]{3,1,2,0:T(8,128)(2,1)} copy(bf16[64,64,2,128]{3,0,2,1:T(8,128)(2,1)S(1)} %fusion.79) | data formatting | bytes 4194304 | tf_op jit(solution)/shard_map/mz,czyx->mcyx/dot_general | solution.py:70
  20.1 1.9 collective-permute-start.2
  22.4 3.8 %collective-permute-start.3 = (bf16[64,26,2,1]{0,2,3,1:T(2,128)(2,1)S(1)}, bf16[64,26,2,1]{0,2,3,1:T(2,128)(2,1)S(1)}, u32[]{:S(2)}, u32[]{:S(2)}) collective-permute-start(bf16[64,26,2,1]{0,2,3,1:T(2,128)(2,1)S(1)} %copy.38), channel_id=1, source_target_pairs={{1,0},{2,1},{3,2},{4,3},{5,4},{6,5},{7,6},{8,7},{9,8},{10,9},{11,1... | collective-permute-start | bytes 19976 | tf_op jit(solution)/shard_map/ppermute | solution.py:21
  29.9 3.8 %fusion.72 = (bf16[1,64,24,2,128]{4,1,3,2,0:T(8,128)(2,1)S(1)}, bf16[1,64,24,2,128]{4,1,3,2,0:T(8,128)(2,1)S(1)}, bf16[1,64,24,2,128]{4,1,3,2,0:T(8,128)(2,1)}, ...) fusion(bf16[64,26,2,1]{3,0,2,1:T(8,128)(2,1)S(1)} %copy.39, ...), kind=kLoop, calls=%fused_computation.123 | loop fusion | flops 9437184 | bytes 5583872 | tf_op jit(solution)/shard_map/stack | solution.py:47
  33.6 4.4 %slice_bitcast_fusion.41 = (bf16[1,64,24,2,128]{4,1,0,3,2:T(8,128)(2,1)S(1)}, bf16[1,64,24,2,128]{4,1,3,2,0:T(8,128)(2,1)}, bf16[1,64,24,2,128]{4,1,3,2,0:T(8,12...) fusion(bf16[64,26,4,130]{3,0,2,1:T(8,128)(2,1)S(1)} %fusion.8), kind=kLoop, calls=%fused_computation.177 | loop fusion | bytes 28311552 | tf_op jit(solution)/shard_map/stack | solution.py:47
  50.1 4.5 %collective-permute-start.4 = (bf16[64,1,2,128]{3,0,2,1:T(8,128)(2,1)S(1)}, bf16[64,1,2,128]{3,0,2,1:T(8,128)(2,1)S(1)}, u32[]{:S(2)}, u32[]{:S(2)}) collective-permute-start(bf16[64,1,2,128]{3,0,2,1:T(8,128)(2,1)S(1)} %get-tuple-element.64), channel_id=1, source_target_pairs={{0,16},{16,32},{32,48},{48,64},{64,80},{80,96},{96,112},{112,128},... | collective-permute-start | bytes 98312 | tf_op jit(solution)/shard_map/ppermute | solution.py:19
  56.8 4.4 %collective-permute-done.5 = bf16[64,1,2,128]{3,0,2,1:T(8,128)(2,1)S(1)} collective-permute-done((bf16[64,1,2,128]{3,0,2,1:T(8,128)(2,1)S(1)}, bf16[64,1,2,128]{3,0,2,1:T(8,128)(2,1)S(1)}, u32[]{:S(2)}, u32[]{:S(2)}) %collective-permute-start.5) | collective-permute-done | bytes 32800 | tf_op jit(solution)/shard_map/ppermute | solution.py:21
  62.1 2.0 collective-permute-start.6
  64.5 3.8 %collective-permute-start.7 = (bf16[64,26,2,1]{0,2,3,1:T(2,128)(2,1)S(1)}, bf16[64,26,2,1]{0,2,3,1:T(2,128)(2,1)S(1)}, u32[]{:S(2)}, u32[]{:S(2)}) collective-permute-start(bf16[64,26,2,1]{0,2,3,1:T(2,128)(2,1)S(1)} %copy.57), channel_id=1, source_target_pairs={{1,0},{2,1},{3,2},{4,3},{5,4},{6,5},{7,6},{8,7},{9,8},{10,9},{11,1... | collective-permute-start | bytes 19976 | tf_op jit(solution)/shard_map/ppermute | solution.py:21
  72.2 2.9 %select_maximum_fusion = bf16[64,26,4,130]{3,0,2,1:T(8,128)(2,1)S(1)} fusion(bf16[64,26,2,1]{3,0,2,1:T(8,128)(2,1)} %copy.59, bf16[64,26,2,1]{3,0,2,1:T(8,128)(2,1)} %copy.58, bf16[64,1,2,128]{3,0,2,1:T(8,128)(2,1)S(1)} %collective-permute-done.5, bf16[64,24,2,128]{3,0,2,1:T(8,128)(2,1)} %copy-done.2, bf16[64,1,2,128]{3,0,2,1:T(8,128)(2,1)S(1)} %collective-permute-done.4), kind=kLoop, calls=%fused_computation.4 | loop fusion | flops 15575040 | bytes 2595840 | tf_op jit(solution)/shard_map/concatenate | solution.py:17
  75.1 41.2 %reduce-scatter.2.cloned.1.call-done = bf16[4,64,2,128]{3,1,2,0:T(8,128)(2,1)} async-done(((bf16[64,64,2,128]{3,1,2,0:T(8,128)(2,1)}), bf16[4,64,2,128]{3,1,2,0:T(8,128)(2,1)}) %reduce-scatter.2.cloned.1.call-update) | async-done | bytes 131088 | tf_op jit(solution)/shard_map/reduce_scatter | solution.py:69
  118.0 3.7 %slice_bitcast_fusion.23 = (bf16[1,64,24,2,128]{4,1,3,2,0:T(8,128)(2,1)S(1)}, bf16[1,64,24,2,128]{4,1,3,2,0:T(8,128)(2,1)S(1)}, bf16[1,64,24,2,128]{4,1,3,2,0:T(...) fusion(bf16[64,26,4,130]{3,0,2,1:T(8,128)(2,1)S(1)} %select_max, ...), kind=kLoop, calls=%fused_computation.151 | loop fusion | bytes 28311552 | tf_op jit(solution)/shard_map/stack | solution.py:47
  123.4 1.9 maximum_maximum_fusion
  130.6 1.8 fusion.27
  132.5 1.8 fusion.25
  134.2 1.8 fusion.23
  136.0 1.8 fusion.21
  137.8 1.7 fusion.19
  139.6 1.8 fusion.17
  141.4 60.9 %all-gather.2.cloned.1.call-done = bf16[64,64,2,128]{3,1,2,0:T(8,128)(2,1)} async-done(((bf16[4,64,2,128]{3,1,2,0:T(8,128)(2,1)}), bf16[64,64,2,128]{3,1,2,0:T(8,128)(2,1)}) %all-gather.2.cloned.1.call-update) | async-done | bytes 2097168 | tf_op jit(solution)/shard_map/all_gather | solution.py:83
  202.3 3.6 %fusion.51 = f32[64,2,128,24]{2,3,1,0:T(8,128)S(1)} fusion(bf16[64,64,2,128]{3,1,2,0:T(8,128)(2,1)} %all-gather.2.cloned.1.call-done, f32[24]{0:T(128)S(1)} %add_convert_fusion, f32[64]{0:T(128)S(1)} %fusion.127, pred[64]{0:T(512)(128)(4,1)S(1)} %iota_compare_fusion.2), kind=kOutput, calls=%fused_computation.74 | convolution fusion | flops 50339328 | bytes 3670432 | tf_op jit(solution)/shard_map/mz,mcyx->czyx/dot_general | solution.py:85
  205.9 6.4 %fusion.61 = bf16[64,24,2,128]{3,0,2,1:T(8,128)(2,1)S(1)} fusion(f32[24,2,128,64,1]{2,3,0,1,4:T(8,128)} %fusion.17, f32[24,2,128,64,1]{2,3,0,1,4:T(8,128)} %fusion.19, f32[24,2,128,64,1]{2,3,0,1,4:T(8,128)} %fusion.21, f32[24,2,128,64,1]{2,3,0,1,4:T(8,128)} %fusion.23, f32[24,2,128,64,1]{2,3,0,1,4:T(8,128)} %fusion.25, f32[24,2,128,64,1]{2,3,0,1,4:T(8,128)} %fusion.27, ...), kind=kLoop, calls=%fused_computation.95 | loop fusion | flops 4718592 | bytes 17301504 | tf_op jit(solution)/shard_map/convert_element_type | solution.py:91
  (101 shorter events, 38.6 us)
Async XLA Ops:
  6.5 109.8 %copy-start = (bf16[4,64,64]{2,1,0:T(8,128)(2,1)S(1)}, bf16[4,64,64]{2,1,0:T(8,128)(2,1)}, u32[]{:S(2)}) copy-start(bf16[4,64,64]{2,1,0:T(8,128)(2,1)} %param.7) | copy-start | bytes 98308
  6.5 109.8 %reduce-scatter.2.cloned.1.call-start = ((), (), s32[]{:S(2)}) async-start(), calls=%async_computation.1 | async-start | bytes 2228224 | tf_op jit(solution)/shard_map/reduce_scatter | solution.py:69
  7.9 10.0 %collective-permute-start = (bf16[64,1,2,128]{3,0,2,1:T(8,128)(2,1)S(1)}, bf16[64,1,2,128]{3,0,2,1:T(8,128)(2,1)S(1)}, u32[]{:S(2)}, u32[]{:S(2)}) collective-permute-start(bf16[64,1,2,128]{3,0,2,1:T(8,128)(2,1)S(1)} %get-tuple-element.71), channel_id=1, source_target_pairs={{0,16},{16,32},{32,48},{48,64},{64,80},{80,96},{96,112},{112,128},... | collective-permute-start | bytes 98312 | tf_op jit(solution)/shard_map/ppermute | solution.py:19
  11.8 7.5 %collective-permute-start.1 = (bf16[64,1,2,128]{3,0,2,1:T(8,128)(2,1)S(1)}, bf16[64,1,2,128]{3,0,2,1:T(8,128)(2,1)S(1)}, u32[]{:S(2)}, u32[]{:S(2)}) collective-permute-start(bf16[64,1,2,128]{3,0,2,1:T(8,128)(2,1)S(1)} %get-tuple-element.70), channel_id=1, source_target_pairs={{16,0},{32,16},{48,32},{64,48},{80,64},{96,80},{112,96},{128,112},... | collective-permute-start | bytes 98312 | tf_op jit(solution)/shard_map/ppermute | solution.py:21
  15.1 2.8 %copy-start.4 = (bf16[64,24,2,128]{3,2,1,0:T(2,128)(2,1)S(1)}, bf16[64,24,2,128]{3,2,1,0:T(2,128)(2,1)}, u32[]{:S(2)}) copy-start(bf16[64,24,2,128]{3,2,1,0:T(2,128)(2,1)} %param.4) | copy-start | bytes 2359300
  17.8 184.4 %all-gather.2.cloned.1.call-start = ((), (), s32[]{:S(2)}) async-start(), calls=%async_computation.2 | async-start | bytes 2228224 | tf_op jit(solution)/shard_map/all_gather | solution.py:83
  20.1 7.4 %collective-permute-start.2 = (bf16[64,26,2,1]{0,2,3,1:T(2,128)(2,1)S(1)}, bf16[64,26,2,1]{0,2,3,1:T(2,128)(2,1)S(1)}, u32[]{:S(2)}, u32[]{:S(2)}) collective-permute-start(bf16[64,26,2,1]{0,2,3,1:T(2,128)(2,1)S(1)} %copy.37), channel_id=1, source_target_pairs={{0,1},{1,2},{2,3},{3,4},{4,5},{5,6},{6,7},{7,8},{8,9},{9,10},{10,1... | collective-permute-start | bytes 19976 | tf_op jit(solution)/shard_map/ppermute | solution.py:19
  22.4 5.6 %collective-permute-start.3 = (bf16[64,26,2,1]{0,2,3,1:T(2,128)(2,1)S(1)}, bf16[64,26,2,1]{0,2,3,1:T(2,128)(2,1)S(1)}, u32[]{:S(2)}, u32[]{:S(2)}) collective-permute-start(bf16[64,26,2,1]{0,2,3,1:T(2,128)(2,1)S(1)} %copy.38), channel_id=1, source_target_pairs={{1,0},{2,1},{3,2},{4,3},{5,4},{6,5},{7,6},{8,7},{9,8},{10,9},{11,1... | collective-permute-start | bytes 19976 | tf_op jit(solution)/shard_map/ppermute | solution.py:21
  40.3 1.6 copy-start.10
  40.3 1.8 copy-start.11
  42.1 1.6 copy-start.15
  43.8 1.6 copy-start.19
  50.0 18.3 %copy-start.2 = (bf16[64,24,2,128]{3,0,2,1:T(8,128)(2,1)}, bf16[64,24,2,128]{3,0,2,1:T(8,128)(2,1)S(1)}, u32[]{:S(2)}) copy-start(bf16[64,24,2,128]{3,0,2,1:T(8,128)(2,1)S(1)} %fusion.60) | copy-start | bytes 2359300
  50.1 6.7 %collective-permute-start.4 = (bf16[64,1,2,128]{3,0,2,1:T(8,128)(2,1)S(1)}, bf16[64,1,2,128]{3,0,2,1:T(8,128)(2,1)S(1)}, u32[]{:S(2)}, u32[]{:S(2)}) collective-permute-start(bf16[64,1,2,128]{3,0,2,1:T(8,128)(2,1)S(1)} %get-tuple-element.64), channel_id=1, source_target_pairs={{0,16},{16,32},{32,48},{48,64},{64,80},{80,96},{96,112},{112,128},... | collective-permute-start | bytes 98312 | tf_op jit(solution)/shard_map/ppermute | solution.py:19
  54.6 6.6 %collective-permute-start.5 = (bf16[64,1,2,128]{3,0,2,1:T(8,128)(2,1)S(1)}, bf16[64,1,2,128]{3,0,2,1:T(8,128)(2,1)S(1)}, u32[]{:S(2)}, u32[]{:S(2)}) collective-permute-start(bf16[64,1,2,128]{3,0,2,1:T(8,128)(2,1)S(1)} %get-tuple-element.65), channel_id=1, source_target_pairs={{16,0},{32,16},{48,32},{64,48},{80,64},{96,80},{112,96},{128,112},... | collective-permute-start | bytes 98312 | tf_op jit(solution)/shard_map/ppermute | solution.py:21
  62.1 7.4 %collective-permute-start.6 = (bf16[64,26,2,1]{0,2,3,1:T(2,128)(2,1)S(1)}, bf16[64,26,2,1]{0,2,3,1:T(2,128)(2,1)S(1)}, u32[]{:S(2)}, u32[]{:S(2)}) collective-permute-start(bf16[64,26,2,1]{0,2,3,1:T(2,128)(2,1)S(1)} %copy.56), channel_id=1, source_target_pairs={{0,1},{1,2},{2,3},{3,4},{4,5},{5,6},{6,7},{7,8},{8,9},{9,10},{10,1... | collective-permute-start | bytes 19976 | tf_op jit(solution)/shard_map/ppermute | solution.py:19
  64.5 6.4 %collective-permute-start.7 = (bf16[64,26,2,1]{0,2,3,1:T(2,128)(2,1)S(1)}, bf16[64,26,2,1]{0,2,3,1:T(2,128)(2,1)S(1)}, u32[]{:S(2)}, u32[]{:S(2)}) collective-permute-start(bf16[64,26,2,1]{0,2,3,1:T(2,128)(2,1)S(1)} %copy.57), channel_id=1, source_target_pairs={{1,0},{2,1},{3,2},{4,3},{5,4},{6,5},{7,6},{8,7},{9,8},{10,9},{11,1... | collective-permute-start | bytes 19976 | tf_op jit(solution)/shard_map/ppermute | solution.py:21
  121.7 1.6 copy-start.3
  121.7 1.6 copy-start.6
  121.8 1.7 copy-start.7
  136.0 1.8 copy-start.18
  141.4 64.5 %copy-start.5 = (bf16[64,24,2,128]{3,2,1,0:T(2,128)(2,1)S(1)}, bf16[64,24,2,128]{3,2,1,0:T(2,128)(2,1)}, u32[]{:S(2)}) copy-start(bf16[64,24,2,128]{3,2,1,0:T(2,128)(2,1)} %param.4) | copy-start | bytes 2359300
  202.3 3.6 %copy-start.12 = (f32[24,2,128,64,1]{2,3,0,1,4:T(8,128)S(1)}, f32[24,2,128,64,1]{2,3,0,1,4:T(8,128)}, u32[]{:S(2)}) copy-start(f32[24,2,128,64,1]{2,3,0,1,4:T(8,128)} %fusion.31) | copy-start | bytes 4718596
  205.9 8.1 %copy-start.1 = (bf16[4,64,64]{2,1,0:T(8,128)(2,1)S(1)}, bf16[4,64,64]{2,1,0:T(8,128)(2,1)}, u32[]{:S(2)}) copy-start(bf16[4,64,64]{2,1,0:T(8,128)(2,1)} %param.7) | copy-start | bytes 98308
  (9 other events, 10.9 us)
Sparse Core Ops, SparseCore 0:
  18.0 98.2 reduce-scatter.1
  118.2 84.0 all-gather.1
where the time goes:
time: 221 us
  waiting for transfers between devices  107 us (48%)
  matrix products  29.6 us (13%)
  local copies, waits for them, and re-layouts  27 us (12%)
  starting transfers between devices  22.5 us (10%)
  other arithmetic  20.5 us (9%)
  between operations  13.8 us (6%)
    all_gather x1, waiting for transfers between devices, local(): block_modes = lax.all_gather(mixed, 'depth', axis=0, tiled=True)  60.9 us
    reduce_scatter x1, waiting for transfers between devices, local(): lax.psum_scatter(jnp.einsum('mz,czyx->mcyx', mode_basis(mode_index, depth...  41.2 us
    dot_general x18, matrix products, convolve(): jnp.einsum('eoc,eczyx->ozyx', weights[depth_tap, row_tap], stacked, prefe...  22.2 us
    ppermute x4, starting transfers between devices, extended(): lax.ppermute(tail, axis, [(i, (i + 1) % count) for i in range(ends)])  12.3 us
    another operation x5, local copies, waits for them, and re-layouts, convolve(): jnp.stack([band[:, :, :, col_tap:col_tap + col_cells] for col_tap in rang...  10.7 us
    ppermute x4, starting transfers between devices, extended(): lax.ppermute(head, axis, [((i + 1) % count, i) for i in range(ends)])  10.2 us
    another operation x6, other arithmetic, convolve(): jnp.stack([band[:, :, :, col_tap:col_tap + col_cells] for col_tap in rang...  7.93 us
    convert_element_type x1, other arithmetic, local(): (volume.astype(jnp.float32) + local_part + spectral).astype(jnp.bfloat16)  6.37 us
  transfers between devices with their start and end apart: 10, of which 5 were waited for; matrix products, arithmetic and copies ran while one was open for 26% of the time, Pallas kernels for 0%

commit v1 on v0

v1 whole, which is shorter than its diff:
```python
import math

import jax
import jax.numpy as jnp
import ml_dtypes
import numpy as np
from jax import lax
from jax.experimental import pallas as pl
from jax.experimental.pallas import tpu as pltpu
from jax.sharding import PartitionSpec as P

MODES = 32
M = 2 * MODES
C = 64
ROWS = 128
LANES = 128
CD = 24
NZ = 384
ND = 16
NG = 16
R = 10
XO = LANES // ND
GROUP = 8
MESH = pl.DeviceIdType.MESH
F32 = jnp.float32
BF16 = jnp.bfloat16


def slab_factors():
    mode = np.arange(M)
    k = np.where(mode < MODES, mode, mode - MODES + 1)
    t = k[:, None] * (2 * np.arange(NZ)[None, :] + 1) * (math.pi / (2 * NZ))
    basis = math.sqrt(2.0 / NZ) * np.where((mode < MODES)[:, None], np.cos(t), np.sin(t))
    z = np.arange(CD) - (CD - 1) / 2
    a = np.arange(MODES + 1)[:, None] * z[None, :] * (math.pi / NZ)
    h = np.linalg.svd(np.concatenate([np.cos(a), np.sin(a)]))[2][:R]
    g = np.einsum("msz,rz->msr", basis.reshape(M, ND, CD), h)
    return g.reshape(M, ND * R), h


def constants():
    g, h = slab_factors()
    hk = np.kron(h, np.eye(16)).astype(ml_dtypes.bfloat16)
    gk = np.kron(g, np.eye(XO)).astype(ml_dtypes.bfloat16)
    return hk, np.ascontiguousarray(hk.T), gk, np.ascontiguousarray(gk.T)


def dot(a, b, ca=1, cb=0):
    return lax.dot_general(a, b, (((ca,), (cb,)), ((), ())), preferred_element_type=F32)


def iota(shape, dim):
    return lax.broadcasted_iota(jnp.int32, shape, dim)


def one_hot(mask):
    return jnp.where(mask, 1.0, 0.0).astype(BF16)


def gelu(x):
    inner = math.sqrt(2.0 / math.pi) * (x + 0.044715 * (x * x * x))
    return 0.5 * x * (1.0 + jnp.tanh(inner))


def kernel(
    vol_h, w1_h, w2_h, mw_h, hk_h, hkt_h, gk_h, gkt_h, out,
    vol, wc1, wc2, mw, hk, hkt, gk, gkt,
    vs, hs, wa, wb, acc, eb, rx,
    gb, fs, fr, bs, br, coef, mixed,
    pw, wp, wall, bd,
    load_sem, vol_sem, fss, frs, bss, brs, pss, prs, qss, qrs, hss, hrs,
):
    d = lax.axis_index("depth")
    g = lax.axis_index("gx")
    q = lax.rem(g, GROUP)
    gbase = g - q

    def depth_peer(k):
        return lax.rem(d + k, ND)

    def group_peer(k):
        return gbase + lax.rem(q + k, GROUP)

    loads = [
        pltpu.make_async_copy(s, t, load_sem.at[i])
        for i, (s, t) in enumerate(
            [(mw_h, mw), (hk_h, hk), (w1_h, wc1), (gk_h, gk), (w2_h, wc2), (gkt_h, gkt), (hkt_h, hkt)]
        )
    ]

    def vol_load(z):
        return pltpu.make_async_copy(vol_h.at[:, z], vol.at[z], vol_sem.at[z])

    loads[0].start()
    loads[1].start()

    def start_vol(z, _):
        vol_load(z).start()
        return 0

    lax.fori_loop(0, CD, start_vol, 0)
    for c in loads[2:]:
        c.start()

    barrier = pltpu.get_barrier_semaphore()

    def greet(dd, gg):
        pl.semaphore_signal(barrier, 1, device_id=(dd, gg), device_id_type=MESH)

    def greet_depth(k, _):
        greet(depth_peer(k), g)
        return 0

    lax.fori_loop(1, ND, greet_depth, 0)

    def greet_group(k, _):
        greet(d, group_peer(k))
        return 0

    lax.fori_loop(1, GROUP, greet_group, 0)
    up, down = lax.rem(d + 1, ND), lax.rem(d + ND - 1, ND)
    right, left = lax.rem(g + 1, NG), lax.rem(g + NG - 1, NG)
    greet(d, right)
    greet(d, left)
    for dd in (up, down):
        for gg in (right, left):
            greet(dd, gg)

    row = iota((ROWS, LANES), 0)
    lane = iota((ROWS, LANES), 1)
    eye = one_hot(row == lane)
    perm = one_hot(lane == (row & 1) * C + (row >> 1))
    permt = one_hot(row == (lane & 1) * C + (lane >> 1))

    loads[0].wait()
    eye64 = eye[:C, :C]
    for p in range(2):
        two = mw[2 * p : 2 * p + 2].reshape(2 * C, C)
        pw[C * p : C * (p + 1), :] = dot(eye64, two, 1, 1).astype(BF16)
    piece = pl.ds(pl.multiple_of(q * 16, 16), 16)
    wp[d] = pw[piece, :]

    loads[1].wait()

    def wait_vol(z, _):
        vol_load(z).wait()
        return 0

    lax.fori_loop(0, CD, wait_vol, 0)
    flat = vol.reshape(CD, ROWS, LANES)

    def compress(i, _):
        r0 = pl.multiple_of(i * 32, 32)
        both = [flat[:, pl.ds(r0 + 16 * j, 16), :].reshape(CD * 16, LANES) for j in range(2)]
        res = dot(hk[...], jnp.concatenate(both, axis=1)).astype(BF16)
        for j in range(2):
            gb[:, pl.ds(r0 + 16 * j, 16), :] = res[:, LANES * j : LANES * (j + 1)].reshape(R, 16, LANES)
        return 0

    lax.fori_loop(0, ROWS // 32, compress, 0)

    for p in range(R // 2):
        pair = [dot(gb[2 * p + j], perm, 0, 0).reshape(ND, XO, LANES) for j in range(2)]
        fs[:, 16 * p : 16 * p + 16, :] = jnp.concatenate(pair, axis=1).astype(BF16)
    fr[d] = fs[d]
    vs[1, ROWS : 2 * ROWS, :] = flat[0]
    vs[CD, ROWS : 2 * ROWS, :] = flat[CD - 1]

    pl.semaphore_wait(barrier, ND - 1 + GROUP - 1 + 2 + 4)

    def piece_copy(k):
        t = depth_peer(k)
        return pltpu.make_async_remote_copy(
            pw.at[piece, :], wp.at[d], pss.at[k], prs.at[k], device_id=(t, g), device_id_type=MESH
        )

    def forward_copy(k):
        t = depth_peer(k)
        return pltpu.make_async_remote_copy(
            fs.at[t], fr.at[d], fss.at[k], frs.at[k], device_id=(t, g), device_id_type=MESH
        )

    def back_copy(k):
        t = depth_peer(k)
        return pltpu.make_async_remote_copy(
            bs.at[t], br.at[d], bss.at[k], brs.at[k], device_id=(t, g), device_id_type=MESH
        )

    def gather_copy(k):
        return pltpu.make_async_remote_copy(
            wp, wall.at[q], qss.at[k], qrs.at[k], device_id=(d, group_peer(k)), device_id_type=MESH
        )

    def slab_copies(n, ts):
        mid = pl.ds(ROWS, ROWS)
        for i, (src, dst, dd) in enumerate([(1, CD + 1, down), (CD, 0, up)]):
            yield pltpu.make_async_remote_copy(
                ts.at[src, mid, :], ts.at[dst, mid, :], hss.at[n, i], hrs.at[n, i], device_id=(dd, g), device_id_type=MESH
            )

    def edge_copies(n):
        i = 2
        for side, gg in ((0, left), (1, right)):
            base = 64 * (1 - side)
            for src, rows, dst, dd in ((0, 32, 0, d), (16, 16, 32, up), (0, 16, 48, down)):
                yield pltpu.make_async_remote_copy(
                    eb.at[n, pl.ds(32 * side + src, rows), :],
                    rx.at[n, pl.ds(base + dst, rows), :],
                    hss.at[n, i],
                    hrs.at[n, i],
                    device_id=(dd, gg),
                    device_id_type=MESH,
                )
                i += 1

    def run(lo, hi, make, what):
        def step(k, _):
            getattr(make(k), what)()
            return 0

        lax.fori_loop(lo, hi, step, 0)

    run(1, ND, piece_copy, "start")
    for c in slab_copies(0, vs):
        c.start()
    run(1, ND, forward_copy, "start")

    erow = iota((64, LANES), 0)
    elane = iota((64, LANES), 1)

    def edges_of(z, slab):
        pick = ((erow == z) & (elane == 0)) | ((erow == z + 32) & (elane == LANES - 1))
        return dot(one_hot(pick), slab, 1, 1)

    def spread(ts, zi, slab):
        ts[zi, 0:ROWS, :] = pltpu.roll(slab, 1, 1)
        ts[zi, ROWS : 2 * ROWS, :] = slab
        ts[zi, 2 * ROWS : 3 * ROWS, :] = pltpu.roll(slab, LANES - 1, 1)

    def fill(z, edge):
        slab = flat[z]
        spread(vs, z + 1, slab)
        acc[z] = slab.astype(F32)
        return edge + edges_of(z, slab)

    for z in (0, CD - 1):
        slab = flat[z]
        vs[z + 1, 0:ROWS, :] = pltpu.roll(slab, 1, 1)
        vs[z + 1, 2 * ROWS : 3 * ROWS, :] = pltpu.roll(slab, LANES - 1, 1)
        acc[z] = slab.astype(F32)
    edge = edges_of(0, flat[0]) + edges_of(CD - 1, flat[CD - 1])
    eb[0] = lax.fori_loop(1, CD - 1, fill, edge).astype(BF16)
    for c in edge_copies(0):
        c.start()

    loads[2].wait()
    loads[4].wait()

    def taps(t, _):
        a, e = t // 3, lax.rem(t, 3)

        def halves(w):
            w0, w1, w2 = w[a, 0, e], w[a, 1, e], w[a, 2, e]
            return jnp.concatenate([w1, w0], axis=0), jnp.concatenate([w2, w1], axis=0)

        lo, hi = halves(wc1)
        wa[t] = (dot(lo, permt[:C]) + dot(hi, permt[C:])).astype(BF16)
        lo, hi = halves(wc2)
        both = (dot(lo, eye[:C]) + dot(hi, eye[C:])).astype(BF16)
        wb[t] = dot(perm, both).astype(BF16)
        return 0

    lax.fori_loop(0, 9, taps, 0)

    run(1, ND, piece_copy, "wait")
    wall[q] = wp[...]
    run(1, GROUP, gather_copy, "start")

    def complete(n, ts):
        for c in slab_copies(n, ts):
            c.wait()
        for c in edge_copies(n):
            c.wait()
        for zi, there in ((0, d > 0), (CD + 1, d < ND - 1)):
            slab = ts[zi, ROWS : 2 * ROWS, :].astype(F32) * jnp.where(there, 1.0, 0.0)
            spread(ts, zi, slab.astype(BF16))
        sub = row & 63
        inside = jnp.where(row < 64, g, NG - 1 - g)
        slabs = jnp.where(sub < 32, 1, jnp.where(sub < 48, d, ND - 1 - d))
        keep = jnp.minimum(inside, slabs) > 0
        cells = jnp.where(keep, rx[n].astype(F32), 0.0).astype(BF16)
        columns = dot(eye, cells, 1, 1).astype(BF16)
        wrow = iota((ROWS, 2 * LANES), 0)
        wlane = iota((ROWS, 2 * LANES), 1)

        def patch(zi, _):
            rho = jnp.where(zi == 0, 39, jnp.where(zi == CD + 1, 48, zi - 1))
            put = ((wrow == rho) & (wlane == 0)) | ((wrow == rho + 64) & (wlane == 2 * LANES - 1))
            ins = dot(columns, one_hot(put)).astype(BF16)
            ts[zi, 0:ROWS, :] = jnp.where(lane == 0, ins[:, :LANES], ts[zi, 0:ROWS, :])
            ts[zi, 2 * ROWS : 3 * ROWS, :] = jnp.where(
                lane == LANES - 1, ins[:, LANES:], ts[zi, 2 * ROWS : 3 * ROWS, :]
            )
            return 0

        lax.fori_loop(0, CD + 2, patch, 0)

    def conv_pair(w, ts, z):
        lhs = jnp.concatenate([w[t] for t in range(9)], axis=1)
        rhs = [ts[pl.ds(z + j, 3)].reshape(9 * ROWS, LANES) for j in range(2)]
        return dot(lhs, jnp.concatenate(rhs, axis=1))

    complete(0, vs)

    def first(i, edge):
        z = 2 * i
        hidden = gelu(conv_pair(wa, vs, z)).astype(BF16)
        for j in range(2):
            slab = hidden[:, LANES * j : LANES * (j + 1)]
            spread(hs, z + j + 1, slab)
            edge = edge + edges_of(z + j, slab)
        return edge

    eb[1] = lax.fori_loop(0, CD // 2, first, jnp.zeros((64, LANES), F32)).astype(BF16)
    for c in slab_copies(1, hs):
        c.start()
    for c in edge_copies(1):
        c.start()

    run(1, GROUP, gather_copy, "wait")
    half = iota((C, LANES), 1) < C

    def diagonal(i, _):
        owner, p = i // 2, lax.rem(i, 2)
        w = wall[pl.ds(4 * p, 4), owner].reshape(C, LANES).astype(F32)
        turned = pltpu.roll(w, C, 1)
        top = [jnp.where(half, w, 0.0), jnp.where(half, turned, 0.0)]
        bottom = [jnp.where(half, 0.0, turned), jnp.where(half, 0.0, w)]
        bd[i, 0:C, :] = jnp.concatenate(top, axis=1).astype(BF16)
        bd[i, C : 2 * C, :] = jnp.concatenate(bottom, axis=1).astype(BF16)
        return 0

    lax.fori_loop(0, M // 2, diagonal, 0)

    loads[3].wait()
    loads[5].wait()
    run(1, ND, forward_copy, "wait")
    coef[...] = dot(gk[...], fr[...].reshape(ND * R * XO, LANES)).astype(BF16)

    def mix(i, _):
        rows = pl.ds(pl.multiple_of(16 * i, 16), 16)
        res = dot(coef[rows, :], bd[i])
        mixed[rows, :] = jnp.concatenate([res[:8, :LANES], res[8:, LANES:]], axis=0).astype(BF16)
        return 0

    lax.fori_loop(0, M // 2, mix, 0, unroll=4)
    bs[...] = dot(gkt[...], mixed[...]).astype(BF16).reshape(ND, R * XO, LANES)
    br[d] = bs[d]
    run(1, ND, back_copy, "start")

    complete(1, hs)

    def second(i, _):
        z = 2 * i
        res = conv_pair(wb, hs, z)
        for j in range(2):
            acc[z + j] += res[:, LANES * j : LANES * (j + 1)]
        return 0

    lax.fori_loop(0, CD // 2, second, 0)

    loads[6].wait()
    run(1, ND, back_copy, "wait")
    for p in range(R // 2):
        pair = br[:, 16 * p : 16 * p + 16, :].astype(F32)
        for j in range(2):
            cols = pair[:, XO * j : XO * (j + 1)].reshape(LANES, ROWS).astype(BF16)
            gb[2 * p + j] = dot(perm, cols, 1, 1).astype(BF16)

    def expand(i, _):
        r0 = pl.multiple_of(i * 32, 32)
        both = [gb[:, pl.ds(r0 + 16 * j, 16), :].reshape(R * 16, LANES) for j in range(2)]
        res = dot(hkt[...], jnp.concatenate(both, axis=1))
        for j in range(2):
            rows = pl.ds(r0 + 16 * j, 16)
            total = acc[:, rows, :] + res[:, LANES * j : LANES * (j + 1)].reshape(CD, 16, LANES)
            out[:, rows, :] = total.astype(BF16)
        return 0

    lax.fori_loop(0, ROWS // 32, expand, 0)


def local(volume, conv_first, conv_second, mode_weights):
    vmem = pltpu.VMEM
    dma = pltpu.SemaphoreType.DMA
    hbm = pl.BlockSpec(memory_space=pl.ANY)
    res = pl.pallas_call(
        kernel,
        out_shape=jax.ShapeDtypeStruct((CD, ROWS, LANES), BF16),
        in_specs=[hbm] * 8,
        out_specs=pl.BlockSpec(memory_space=pltpu.VMEM),
        scratch_shapes=[
            vmem((CD, C, 2, LANES), BF16),
            vmem((3, 3, 3, C, C), BF16),
            vmem((3, 3, 3, C, C), BF16),
            vmem((4, C, C), BF16),
            vmem((R * 16, CD * 16), BF16),
            vmem((CD * 16, R * 16), BF16),
            vmem((M * XO, ND * R * XO), BF16),
            vmem((ND * R * XO, M * XO), BF16),
            vmem((CD + 2, 3 * ROWS, LANES), BF16),
            vmem((CD + 2, 3 * ROWS, LANES), BF16),
            vmem((9, ROWS, LANES), BF16),
            vmem((9, ROWS, LANES), BF16),
            vmem((CD, ROWS, LANES), F32),
            vmem((2, 64, LANES), BF16),
            vmem((2, ROWS, LANES), BF16),
            vmem((R, ROWS, LANES), BF16),
            vmem((ND, R * XO, LANES), BF16),
            vmem((ND, R * XO, LANES), BF16),
            vmem((ND, R * XO, LANES), BF16),
            vmem((ND, R * XO, LANES), BF16),
            vmem((M * XO, LANES), BF16),
            vmem((M * XO, LANES), BF16),
            vmem((2 * C, LANES), BF16),
            vmem((ND, 16, LANES), BF16),
            vmem((GROUP, ND, 16, LANES), BF16),
            vmem((M // 2, ROWS, 2 * LANES), BF16),
            dma((7,)),
            dma((CD,)),
            dma((ND,)),
            dma((ND,)),
            dma((ND,)),
            dma((ND,)),
            dma((ND,)),
            dma((ND,)),
            dma((GROUP,)),
            dma((GROUP,)),
            dma((2, 8)),
            dma((2, 8)),
        ],
        compiler_params=pltpu.CompilerParams(
            collective_id=0, has_side_effects=True, vmem_limit_bytes=48 * 2**20
        ),
    )(volume, conv_first, conv_second, mode_weights, *constants())
    return res.reshape(CD, C, 2, LANES).transpose(1, 0, 2, 3)


def solution(mesh):
    placed = (P(None, "depth", None, "gx"), P(), P(), P("depth", None, None))
    return jax.shard_map(
        local, mesh=mesh, in_specs=placed, out_specs=P(None, "depth", None, "gx"), check_vma=False
    )
```

time: 221 us -> 61.4 us (0.28)
  the two profiles are of different devices: /device:TPU:16 before, /device:TPU:1 now
where the time goes in v1:
time: 61.4 us; the launch traced here: 61 us
  Pallas kernels  51.1 us (83%)
  local copies, waits for them, and re-layouts  9.88 us (16%)
    pallas_call x1, Pallas kernels, local(): pl.pallas_call(kernel, out_shape=jax.ShapeDtypeStruct((CD, ROWS, LANES),...  51.1 us
    unnamed x16, local copies, waits for them, and re-layouts  8.46 us
    reshape x1, local copies, waits for them, and re-layouts, local(): return res.reshape(CD, C, 2, LANES).transpose(1, 0, 2, 3)  1.42 us

profile of v1, /device:TPU:1, one launch (start us, length us, event | category | flops | bytes accessed | tf_op | source)
XLA Modules:
  0.0 61.0 jit_solution(13713917565457262207)
XLA Ops:
  0.0 0.0 copy-start
  0.0 1.3 %copy-done = bf16[1280,512]{1,0:T(8,128)(2,1)S(1)} copy-done((bf16[1280,512]{1,0:T(8,128)(2,1)S(1)}, bf16[1280,512]{1,0:T(8,128)(2,1)}, u32[]{:S(2)}) %copy-start) | copy-done | bytes 1310744
  1.3 0.0 copy-start.1
  1.3 1.3 %copy-done.1 = bf16[512,1280]{1,0:T(8,128)(2,1)S(1)} copy-done((bf16[512,1280]{1,0:T(8,128)(2,1)S(1)}, bf16[512,1280]{1,0:T(8,128)(2,1)}, u32[]{:S(2)}) %copy-start.1) | copy-done | bytes 1310744
  2.6 0.0 copy-start.2
  2.6 1.1 %copy-done.2 = bf16[64,24,2,128]{3,2,1,0:T(2,128)(2,1)S(1)} copy-done((bf16[64,24,2,128]{3,2,1,0:T(2,128)(2,1)S(1)}, bf16[64,24,2,128]{3,2,1,0:T(2,128)(2,1)}, u32[]{:S(2)}) %copy-start.2) | copy-done | bytes 786456
  3.8 0.0 copy-start.3
  3.8 1.0 %copy-done.3 = bf16[3,3,3,64,64]{4,3,2,1,0:T(8,128)(2,1)S(1)} copy-done((bf16[3,3,3,64,64]{4,3,2,1,0:T(8,128)(2,1)S(1)}, bf16[3,3,3,64,64]{4,3,2,1,0:T(8,128)(2,1)}, u32[]{:S(2)}) %copy-start.3) | copy-done | bytes 221208
  4.8 0.0 copy-start.4
  4.8 1.0 %copy-done.4 = bf16[3,3,3,64,64]{4,3,2,1,0:T(8,128)(2,1)S(1)} copy-done((bf16[3,3,3,64,64]{4,3,2,1,0:T(8,128)(2,1)S(1)}, bf16[3,3,3,64,64]{4,3,2,1,0:T(8,128)(2,1)}, u32[]{:S(2)}) %copy-start.4) | copy-done | bytes 221208
  5.8 0.0 copy-start.5
  5.8 0.9 %copy-done.5 = bf16[384,160]{1,0:T(8,128)(2,1)S(1)} copy-done((bf16[384,160]{1,0:T(8,128)(2,1)S(1)}, bf16[384,160]{1,0:T(8,128)(2,1)}, u32[]{:S(2)}) %copy-start.5) | copy-done | bytes 122904
  6.7 0.0 copy-start.6
  6.7 0.9 %copy-done.6 = bf16[160,384]{1,0:T(8,128)(2,1)S(1)} copy-done((bf16[160,384]{1,0:T(8,128)(2,1)S(1)}, bf16[160,384]{1,0:T(8,128)(2,1)}, u32[]{:S(2)}) %copy-start.6) | copy-done | bytes 122904
  7.6 0.0 copy-start.7
  7.6 0.8 %copy-done.7 = bf16[4,64,64]{2,1,0:T(8,128)(2,1)S(1)} copy-done((bf16[4,64,64]{2,1,0:T(8,128)(2,1)S(1)}, bf16[4,64,64]{2,1,0:T(8,128)(2,1)}, u32[]{:S(2)}) %copy-start.7) | copy-done | bytes 32792
  8.5 51.1 %shard_map.82 = bf16[24,128,128]{2,1,0:T(8,128)(2,1)S(1)} custom-call(bf16[64,24,2,128]{3,2,1,0:T(2,128)(2,1)S(1)} %copy-done.2, bf16[3,3,3,64,64]{4,3,2,1,0:T(8,128)(2,1)S(1)} %copy-done.3, bf16[3,3,3,64,64]{4,3,2,1,0:T(8,128)(2,1)S(1)} %copy-done.4, bf16[4,64,64]{2,1,0:T(8,128)(2,1)S(1)} %copy-done.7, bf16[160,384]{1,0:T(8,128)(2,1)S(1)} %copy-done.6, ...), custom_call_target="tpu_custom_call" | custom-call | tf_op jit(solution)/shard_map/pallas_call | solution.py:397
  59.6 1.4 %copy.11 = bf16[24,64,2,128]{3,2,0,1:T(2,128)(2,1)} copy(bf16[24,64,2,128]{3,2,1,0:T(2,128)(2,1)S(1)} %bitcast.4) | data formatting | bytes 1572864 | tf_op jit(solution)/shard_map/reshape | solution.py:446
Async XLA Ops:
  0.0 1.3 %copy-start = (bf16[1280,512]{1,0:T(8,128)(2,1)S(1)}, bf16[1280,512]{1,0:T(8,128)(2,1)}, u32[]{:S(2)}) copy-start(bf16[1280,512]{1,0:T(8,128)(2,1)} %constant.11.clone.gkt_h) | copy-start | bytes 3932164
  1.3 1.3 %copy-start.1 = (bf16[512,1280]{1,0:T(8,128)(2,1)S(1)}, bf16[512,1280]{1,0:T(8,128)(2,1)}, u32[]{:S(2)}) copy-start(bf16[512,1280]{1,0:T(8,128)(2,1)} %constant.10.clone.gk_h) | copy-start | bytes 3932164
  2.6 1.1 %copy-start.2 = (bf16[64,24,2,128]{3,2,1,0:T(2,128)(2,1)S(1)}, bf16[64,24,2,128]{3,2,1,0:T(2,128)(2,1)}, u32[]{:S(2)}) copy-start(bf16[64,24,2,128]{3,2,1,0:T(2,128)(2,1)} %vol_h.1) | copy-start | bytes 2359300
  3.8 1.0 %copy-start.3 = (bf16[3,3,3,64,64]{4,3,2,1,0:T(8,128)(2,1)S(1)}, bf16[3,3,3,64,64]{4,3,2,1,0:T(8,128)(2,1)}, u32[]{:S(2)}) copy-start(bf16[3,3,3,64,64]{4,3,2,1,0:T(8,128)(2,1)} %w1_h.1) | copy-start | bytes 663556
  4.8 1.0 %copy-start.4 = (bf16[3,3,3,64,64]{4,3,2,1,0:T(8,128)(2,1)S(1)}, bf16[3,3,3,64,64]{4,3,2,1,0:T(8,128)(2,1)}, u32[]{:S(2)}) copy-start(bf16[3,3,3,64,64]{4,3,2,1,0:T(8,128)(2,1)} %w2_h.1) | copy-start | bytes 663556
  5.8 0.9 %copy-start.5 = (bf16[384,160]{1,0:T(8,128)(2,1)S(1)}, bf16[384,160]{1,0:T(8,128)(2,1)}, u32[]{:S(2)}) copy-start(bf16[384,160]{1,0:T(8,128)(2,1)} %constant.9.clone.hkt_h) | copy-start | bytes 368644
  6.7 0.9 %copy-start.6 = (bf16[160,384]{1,0:T(8,128)(2,1)S(1)}, bf16[160,384]{1,0:T(8,128)(2,1)}, u32[]{:S(2)}) copy-start(bf16[160,384]{1,0:T(8,128)(2,1)} %constant.8.clone.hk_h) | copy-start | bytes 368644
  7.6 0.8 %copy-start.7 = (bf16[4,64,64]{2,1,0:T(8,128)(2,1)S(1)}, bf16[4,64,64]{2,1,0:T(8,128)(2,1)}, u32[]{:S(2)}) copy-start(bf16[4,64,64]{2,1,0:T(8,128)(2,1)} %mw_h.1) | copy-start | bytes 98308

commit v2 on v1

--- a/solution.py
+++ b/solution.py
@@ -20,7 +20,6 @@
 NG = 16
 R = 10
 XO = LANES // ND
-GROUP = 8
 MESH = pl.DeviceIdType.MESH
 F32 = jnp.float32
 BF16 = jnp.bfloat16
@@ -67,19 +66,28 @@
     vol, wc1, wc2, mw, hk, hkt, gk, gkt,
     vs, hs, wa, wb, acc, eb, rx,
     gb, fs, fr, bs, br, coef, mixed,
-    pw, wp, wall, bd,
-    load_sem, vol_sem, fss, frs, bss, brs, pss, prs, qss, qrs, hss, hrs,
+    wall, bd, res_out,
+    load_sem, vol_sem, fss, frs, bss, brs, pss, prs, hss, hrs, out_sem,
 ):
     d = lax.axis_index("depth")
     g = lax.axis_index("gx")
-    q = lax.rem(g, GROUP)
-    gbase = g - q
+    xd, zd = d // 4, lax.rem(d, 4)
+    core = lax.rem(g, 2)
+    half_z = zd // 2
 
     def depth_peer(k):
         return lax.rem(d + k, ND)
 
-    def group_peer(k):
-        return gbase + lax.rem(q + k, GROUP)
+    def z_peer(k):
+        return xd * 4 + lax.rem(zd + k, 4)
+
+    def x_peer(k):
+        return lax.rem(xd + k, 4) * 4 + zd
+
+    def far_first(j):
+        other = 1 - j // 8
+        z = 2 * (half_z + other * (1 - 2 * half_z)) + lax.rem(zd + j + 1, 2)
+        return lax.rem(xd + 1 + lax.rem(j, 8) // 2, 4) * 4 + z
 
     loads = [
         pltpu.make_async_copy(s, t, load_sem.at[i])
@@ -113,11 +121,8 @@
 
     lax.fori_loop(1, ND, greet_depth, 0)
 
-    def greet_group(k, _):
-        greet(d, group_peer(k))
-        return 0
-
-    lax.fori_loop(1, GROUP, greet_group, 0)
+    twin = g + 1 - 2 * core
+    greet(d, twin)
     up, down = lax.rem(d + 1, ND), lax.rem(d + ND - 1, ND)
     right, left = lax.rem(g + 1, NG), lax.rem(g + NG - 1, NG)
     greet(d, right)
@@ -133,63 +138,33 @@
     permt = one_hot(row == (lane & 1) * C + (lane >> 1))
 
     loads[0].wait()
-    eye64 = eye[:C, :C]
-    for p in range(2):
-        two = mw[2 * p : 2 * p + 2].reshape(2 * C, C)
-        pw[C * p : C * (p + 1), :] = dot(eye64, two, 1, 1).astype(BF16)
-    piece = pl.ds(pl.multiple_of(q * 16, 16), 16)
-    wp[d] = pw[piece, :]
-
-    loads[1].wait()
-
-    def wait_vol(z, _):
-        vol_load(z).wait()
-        return 0
-
-    lax.fori_loop(0, CD, wait_vol, 0)
-    flat = vol.reshape(CD, ROWS, LANES)
-
-    def compress(i, _):
-        r0 = pl.multiple_of(i * 32, 32)
-        both = [flat[:, pl.ds(r0 + 16 * j, 16), :].reshape(CD * 16, LANES) for j in range(2)]
-        res = dot(hk[...], jnp.concatenate(both, axis=1)).astype(BF16)
-        for j in range(2):
-            gb[:, pl.ds(r0 + 16 * j, 16), :] = res[:, LANES * j : LANES * (j + 1)].reshape(R, 16, LANES)
-        return 0
-
-    lax.fori_loop(0, ROWS // 32, compress, 0)
-
-    for p in range(R // 2):
-        pair = [dot(gb[2 * p + j], perm, 0, 0).reshape(ND, XO, LANES) for j in range(2)]
-        fs[:, 16 * p : 16 * p + 16, :] = jnp.concatenate(pair, axis=1).astype(BF16)
-    fr[d] = fs[d]
-    vs[1, ROWS : 2 * ROWS, :] = flat[0]
-    vs[CD, ROWS : 2 * ROWS, :] = flat[CD - 1]
-
-    pl.semaphore_wait(barrier, ND - 1 + GROUP - 1 + 2 + 4)
-
-    def piece_copy(k):
-        t = depth_peer(k)
+    two = mw[pl.ds(2 * core, 2)].reshape(2 * C, C)
+    wall[core, xd, zd] = dot(eye[:C, :C], two, 1, 1).astype(BF16)
+
+    def weights_copy(n, k):
+        ref = [wall.at[core, xd, zd], wall.at[core, xd], wall.at[core]][n]
+        to = [(z_peer(k), g), (x_peer(k), g), (d, twin)][n]
         return pltpu.make_async_remote_copy(
-            pw.at[piece, :], wp.at[d], pss.at[k], prs.at[k], device_id=(t, g), device_id_type=MESH
+            ref, ref, pss.at[n, k], prs.at[n, k], device_id=to, device_id_type=MESH
         )
 
-    def forward_copy(k):
-        t = depth_peer(k)
+    def weights_from(n, k):
+        ref = [
+            wall.at[core, xd, lax.rem(zd + 4 - k, 4)],
+            wall.at[core, lax.rem(xd + 4 - k, 4)],
+            wall.at[1 - core],
+        ][n]
         return pltpu.make_async_remote_copy(
-            fs.at[t], fr.at[d], fss.at[k], frs.at[k], device_id=(t, g), device_id_type=MESH
+            ref, ref, pss.at[n, k], prs.at[n, k], device_id=(d, twin), device_id_type=MESH
         )
 
-    def back_copy(k):
-        t = depth_peer(k)
-        return pltpu.make_async_remote_copy(
-            bs.at[t], br.at[d], bss.at[k], brs.at[k], device_id=(t, g), device_id_type=MESH
-        )
-
-    def gather_copy(k):
-        return pltpu.make_async_remote_copy(
-            wp, wall.at[q], qss.at[k], qrs.at[k], device_id=(d, group_peer(k)), device_id_type=MESH
-        )
+    def weights_start(n):
+        for k in range(1, 4 if n < 2 else 2):
+            weights_copy(n, k).start()
+
+    def weights_wait(n):
+        for k in range(1, 4 if n < 2 else 2):
+            weights_from(n, k).wait()
 
     def slab_copies(n, ts):
         mid = pl.ds(ROWS, ROWS)
@@ -213,46 +188,82 @@
                 )
                 i += 1
 
-    def run(lo, hi, make, what):
-        def step(k, _):
-            getattr(make(k), what)()
-            return 0
-
-        lax.fori_loop(lo, hi, step, 0)
-
-    run(1, ND, piece_copy, "start")
-    for c in slab_copies(0, vs):
-        c.start()
-    run(1, ND, forward_copy, "start")
-
+
+    def wait_vol(z, _):
+        vol_load(z).wait()
+        return 0
+
+    lax.fori_loop(0, CD, wait_vol, 0)
+    flat = vol.reshape(CD, ROWS, LANES)
     erow = iota((64, LANES), 0)
     elane = iota((64, LANES), 1)
 
     def edges_of(z, slab):
         pick = ((erow == z) & (elane == 0)) | ((erow == z + 32) & (elane == LANES - 1))
         return dot(one_hot(pick), slab, 1, 1)
+
+    def edge_step(z, edge):
+        return edge + edges_of(z, flat[z])
+
+    eb[0] = lax.fori_loop(0, CD, edge_step, jnp.zeros((64, LANES), F32), unroll=12).astype(BF16)
+    vs[1, ROWS : 2 * ROWS, :] = flat[0]
+    vs[CD, ROWS : 2 * ROWS, :] = flat[CD - 1]
+    loads[1].wait()
+
+
+    def compress(i, _):
+        r0 = pl.multiple_of(i * 32, 32)
+        both = [flat[:, pl.ds(r0 + 16 * j, 16), :].reshape(CD * 16, LANES) for j in range(2)]
+        res = dot(hk[...], jnp.concatenate(both, axis=1)).astype(BF16)
+        for j in range(2):
+            gb[:, pl.ds(r0 + 16 * j, 16), :] = res[:, LANES * j : LANES * (j + 1)].reshape(R, 16, LANES)
+        return 0
+
+    lax.fori_loop(0, ROWS // 32, compress, 0, unroll=4)
+
+    for p in range(R // 2):
+        pair = [dot(gb[2 * p + j], perm, 0, 0).reshape(ND, XO, LANES) for j in range(2)]
+        fs[:, 16 * p : 16 * p + 16, :] = jnp.concatenate(pair, axis=1).astype(BF16)
+    fr[d] = fs[d]
+
+
+    def spectral_copy(src, dst, send, recv, t):
+        return pltpu.make_async_remote_copy(
+            src.at[t], dst.at[d], send.at[t], recv.at[d], device_id=(t, g), device_id_type=MESH
+        )
+
+    def spectral_from(src, dst, send, recv, t):
+        return pltpu.make_async_remote_copy(
+            src.at[t], dst.at[t], send.at[t], recv.at[t], device_id=(t, g), device_id_type=MESH
+        )
+
+    pl.semaphore_wait(barrier, ND - 1 + 1 + 2 + 4)
+    weights_start(0)
+    for c in edge_copies(0):
+        c.start()
+    for c in slab_copies(0, vs):
+        c.start()
+
+    def send_forward(j, _):
+        spectral_copy(fs, fr, fss, frs, far_first(j)).start()
+        return 0
+
+    lax.fori_loop(0, ND - 1, send_forward, 0)
 
     def spread(ts, zi, slab):
         ts[zi, 0:ROWS, :] = pltpu.roll(slab, 1, 1)
         ts[zi, ROWS : 2 * ROWS, :] = slab
         ts[zi, 2 * ROWS : 3 * ROWS, :] = pltpu.roll(slab, LANES - 1, 1)
 
-    def fill(z, edge):
-        slab = flat[z]
-        spread(vs, z + 1, slab)
-        acc[z] = slab.astype(F32)
-        return edge + edges_of(z, slab)
+    def fill(z, _):
+        spread(vs, z + 1, flat[z])
+        return 0
 
     for z in (0, CD - 1):
         slab = flat[z]
         vs[z + 1, 0:ROWS, :] = pltpu.roll(slab, 1, 1)
         vs[z + 1, 2 * ROWS : 3 * ROWS, :] = pltpu.roll(slab, LANES - 1, 1)
-        acc[z] = slab.astype(F32)
-    edge = edges_of(0, flat[0]) + edges_of(CD - 1, flat[CD - 1])
-    eb[0] = lax.fori_loop(1, CD - 1, fill, edge).astype(BF16)
-    for c in edge_copies(0):
-        c.start()
-
+    lax.fori_loop(1, CD - 1, fill, 0, unroll=11)
     loads[2].wait()
     loads[4].wait()
 
@@ -270,11 +281,8 @@
         wb[t] = dot(perm, both).astype(BF16)
         return 0
 
-    lax.fori_loop(0, 9, taps, 0)
-
-    run(1, ND, piece_copy, "wait")
-    wall[q] = wp[...]
-    run(1, GROUP, gather_copy, "start")
+    lax.fori_loop(0, 9, taps, 0, unroll=3)
+
 
     def complete(n, ts):
         for c in slab_copies(n, ts):
@@ -303,14 +311,18 @@
             )
             return 0
 
-        lax.fori_loop(0, CD + 2, patch, 0)
+        lax.fori_loop(0, CD + 2, patch, 0, unroll=13)
 
     def conv_pair(w, ts, z):
         lhs = jnp.concatenate([w[t] for t in range(9)], axis=1)
         rhs = [ts[pl.ds(z + j, 3)].reshape(9 * ROWS, LANES) for j in range(2)]
         return dot(lhs, jnp.concatenate(rhs, axis=1))
 
+    weights_wait(0)
+    weights_start(1)
     complete(0, vs)
+    weights_wait(1)
+    weights_start(2)
 
     def first(i, edge):
         z = 2 * i
@@ -321,30 +333,39 @@
             edge = edge + edges_of(z + j, slab)
         return edge
 
-    eb[1] = lax.fori_loop(0, CD // 2, first, jnp.zeros((64, LANES), F32)).astype(BF16)
+    eb[1] = lax.fori_loop(0, CD // 2, first, jnp.zeros((64, LANES), F32), unroll=2).astype(BF16)
     for c in slab_copies(1, hs):
         c.start()
     for c in edge_copies(1):
         c.start()
 
-    run(1, GROUP, gather_copy, "wait")
     half = iota((C, LANES), 1) < C
 
-    def diagonal(i, _):
-        owner, p = i // 2, lax.rem(i, 2)
-        w = wall[pl.ds(4 * p, 4), owner].reshape(C, LANES).astype(F32)
-        turned = pltpu.roll(w, C, 1)
-        top = [jnp.where(half, w, 0.0), jnp.where(half, turned, 0.0)]
-        bottom = [jnp.where(half, 0.0, turned), jnp.where(half, 0.0, w)]
-        bd[i, 0:C, :] = jnp.concatenate(top, axis=1).astype(BF16)
-        bd[i, C : 2 * C, :] = jnp.concatenate(bottom, axis=1).astype(BF16)
-        return 0
-
-    lax.fori_loop(0, M // 2, diagonal, 0)
+    def diagonal(p):
+        def step(owner, _):
+            i = 2 * owner + p
+            w = wall[p, owner // 4, lax.rem(owner, 4)].astype(F32)
+            turned = pltpu.roll(w, C, 1)
+            top = [jnp.where(half, w, 0.0), jnp.where(half, turned, 0.0)]
+            bottom = [jnp.where(half, 0.0, turned), jnp.where(half, 0.0, w)]
+            bd[i, 0:C, :] = jnp.concatenate(top, axis=1).astype(BF16)
+            bd[i, C : 2 * C, :] = jnp.concatenate(bottom, axis=1).astype(BF16)
+            return 0
+
+        return step
+
+    lax.fori_loop(0, ND, diagonal(core), 0, unroll=4)
+    weights_wait(2)
+    lax.fori_loop(0, ND, diagonal(1 - core), 0, unroll=4)
 
     loads[3].wait()
     loads[5].wait()
-    run(1, ND, forward_copy, "wait")
+
+    def wait_forward(k, _):
+        spectral_from(fs, fr, fss, frs, depth_peer(k)).wait()
+        return 0
+
+    lax.fori_loop(1, ND, wait_forward, 0)
     coef[...] = dot(gk[...], fr[...].reshape(ND * R * XO, LANES)).astype(BF16)
 
     def mix(i, _):
@@ -353,10 +374,23 @@
         mixed[rows, :] = jnp.concatenate([res[:8, :LANES], res[8:, LANES:]], axis=0).astype(BF16)
         return 0
 
-    lax.fori_loop(0, M // 2, mix, 0, unroll=4)
-    bs[...] = dot(gkt[...], mixed[...]).astype(BF16).reshape(ND, R * XO, LANES)
+    lax.fori_loop(0, M // 2, mix, 0, unroll=8)
+    def send_back(xs, count):
+        n = 4 * R * XO
+        rows = pl.ds(pl.multiple_of(xs * n, 16), n)
+        bs[pl.ds(xs * 4, 4)] = dot(gkt[rows, :], mixed[...]).astype(BF16).reshape(4, R * XO, LANES)
+
+        def step(j, _):
+            far = half_z + (1 - j // 2) * (1 - 2 * half_z)
+            spectral_copy(bs, br, bss, brs, xs * 4 + 2 * far + lax.rem(zd + j + 1, 2)).start()
+            return 0
+
+        lax.fori_loop(0, count, step, 0)
+
+    for k in (2, 1, 3):
+        send_back(lax.rem(xd + k, 4), 4)
+    send_back(xd, 3)
     br[d] = bs[d]
-    run(1, ND, back_copy, "start")
 
     complete(1, hs)
 
@@ -364,13 +398,18 @@
         z = 2 * i
         res = conv_pair(wb, hs, z)
         for j in range(2):
-            acc[z + j] += res[:, LANES * j : LANES * (j + 1)]
-        return 0
-
-    lax.fori_loop(0, CD // 2, second, 0)
+            acc[z + j] = flat[z + j].astype(F32) + res[:, LANES * j : LANES * (j + 1)]
+        return 0
+
+    lax.fori_loop(0, CD // 2, second, 0, unroll=2)
 
     loads[6].wait()
-    run(1, ND, back_copy, "wait")
+
+    def wait_back(k, _):
+        spectral_from(bs, br, bss, brs, depth_peer(k)).wait()
+        return 0
+
+    lax.fori_loop(1, ND, wait_back, 0)
     for p in range(R // 2):
         pair = br[:, 16 * p : 16 * p + 16, :].astype(F32)
         for j in range(2):
@@ -384,21 +423,29 @@
         for j in range(2):
             rows = pl.ds(r0 + 16 * j, 16)
             total = acc[:, rows, :] + res[:, LANES * j : LANES * (j + 1)].reshape(CD, 16, LANES)
-            out[:, rows, :] = total.astype(BF16)
-        return 0
-
-    lax.fori_loop(0, ROWS // 32, expand, 0)
+            res_out[:, rows, :] = total.astype(BF16)
+            put_out(i, j).start()
+        return 0
+
+    def put_out(i, j):
+        rows = pl.ds(pl.multiple_of(i * 32, 32) + 16 * j, 16)
+        return pltpu.make_async_copy(res_out.at[:, rows, :], out.at[:, rows, :], out_sem.at[2 * i + j])
+
+    lax.fori_loop(0, ROWS // 32, expand, 0, unroll=4)
+    for i in range(ROWS // 32):
+        for j in range(2):
+            put_out(i, j).wait()
 
 
 def local(volume, conv_first, conv_second, mode_weights):
     vmem = pltpu.VMEM
     dma = pltpu.SemaphoreType.DMA
-    hbm = pl.BlockSpec(memory_space=pl.ANY)
+    hbm = pl.BlockSpec(memory_space=pltpu.HBM)
     res = pl.pallas_call(
         kernel,
         out_shape=jax.ShapeDtypeStruct((CD, ROWS, LANES), BF16),
         in_specs=[hbm] * 8,
-        out_specs=pl.BlockSpec(memory_space=pltpu.VMEM),
+        out_specs=pl.BlockSpec(memory_space=pltpu.HBM),
         scratch_shapes=[
             vmem((CD, C, 2, LANES), BF16),
             vmem((3, 3, 3, C, C), BF16),
@@ -422,25 +469,23 @@
             vmem((ND, R * XO, LANES), BF16),
             vmem((M * XO, LANES), BF16),
             vmem((M * XO, LANES), BF16),
-            vmem((2 * C, LANES), BF16),
-            vmem((ND, 16, LANES), BF16),
-            vmem((GROUP, ND, 16, LANES), BF16),
+            vmem((2, 4, 4, C, LANES), BF16),
             vmem((M // 2, ROWS, 2 * LANES), BF16),
+            vmem((CD, ROWS, LANES), BF16),
             dma((7,)),
             dma((CD,)),
             dma((ND,)),
             dma((ND,)),
             dma((ND,)),
             dma((ND,)),
-            dma((ND,)),
-            dma((ND,)),
-            dma((GROUP,)),
-            dma((GROUP,)),
+            dma((3, 4)),
+            dma((3, 4)),
             dma((2, 8)),
             dma((2, 8)),
+            dma((8,)),
         ],
         compiler_params=pltpu.CompilerParams(
-            collective_id=0, has_side_effects=True, vmem_limit_bytes=48 * 2**20
+            collective_id=0, has_side_effects=True, vmem_limit_bytes=60 * 2**20
         ),
     )(volume, conv_first, conv_second, mode_weights, *constants())
     return res.reshape(CD, C, 2, LANES).transpose(1, 0, 2, 3)

time: 61.4 us -> 40.5 us (0.66)
  Pallas kernels: 51.1 us -> 37.8 us
  local copies, waits for them, and re-layouts: 9.88 us -> 2.55 us
    pallas_call x1, Pallas kernels: 51.1 us -> 37.8 us  [local(): pl.pallas_call(kernel, out_shape=jax.ShapeDtypeStruct((CD, ROWS, LANES),...]
    unnamed x16 -> x0, local copies, waits for them, and re-layouts: 8.46 us -> none
    reshape x1, local copies, waits for them, and re-layouts: 1.42 us -> 2.55 us  [local(): return res.reshape(CD, C, 2, LANES).transpose(1, 0, 2, 3)]
where the time goes in v2:
time: 40.5 us; the launch traced here: 40.4 us
  Pallas kernels  37.8 us (93%)
  local copies, waits for them, and re-layouts  2.55 us (6%)
    pallas_call x1, Pallas kernels, local(): pl.pallas_call(kernel, out_shape=jax.ShapeDtypeStruct((CD, ROWS, LANES),...  37.8 us
    reshape x1, local copies, waits for them, and re-layouts, local(): return res.reshape(CD, C, 2, LANES).transpose(1, 0, 2, 3)  2.55 us

profile of v2, /device:TPU:1, one launch (start us, length us, event | category | flops | bytes accessed | tf_op | source)
XLA Modules:
  0.0 40.4 jit_solution(7624048888269421636)
XLA Ops:
  0.0 37.8 %shard_map.82 = bf16[24,128,128]{2,1,0:T(8,128)(2,1)} custom-call(bf16[64,24,2,128]{3,2,1,0:T(2,128)(2,1)} %vol_h.1, bf16[3,3,3,64,64]{4,3,2,1,0:T(8,128)(2,1)} %w1_h.1, bf16[3,3,3,64,64]{4,3,2,1,0:T(8,128)(2,1)} %w2_h.1, bf16[4,64,64]{2,1,0:T(8,128)(2,1)} %mw_h.1, bf16[160,384]{1,0:T(8,128)(2,1)} %constant.8.clone.hk_h, ...), custom_call_target="tpu_custom_call" | custom-call | tf_op jit(solution)/shard_map/pallas_call | solution.py:444
  37.8 2.6 %copy.11 = bf16[24,64,2,128]{3,2,0,1:T(2,128)(2,1)} copy(bf16[24,64,2,128]{3,2,1,0:T(2,128)(2,1)} %bitcast.4) | data formatting | bytes 1572864 | tf_op jit(solution)/shard_map/reshape | solution.py:491

commit v3 on v2

--- a/solution.py
+++ b/solution.py
@@ -122,7 +122,8 @@
     lax.fori_loop(1, ND, greet_depth, 0)
 
     twin = g + 1 - 2 * core
-    greet(d, twin)
+    for k in range(4):
+        greet(x_peer(k), twin)
     up, down = lax.rem(d + 1, ND), lax.rem(d + ND - 1, ND)
     right, left = lax.rem(g + 1, NG), lax.rem(g + NG - 1, NG)
     greet(d, right)
@@ -142,28 +143,27 @@
     wall[core, xd, zd] = dot(eye[:C, :C], two, 1, 1).astype(BF16)
 
     def weights_copy(n, k):
-        ref = [wall.at[core, xd, zd], wall.at[core, xd], wall.at[core]][n]
-        to = [(z_peer(k), g), (x_peer(k), g), (d, twin)][n]
+        ref = wall.at[core, xd, zd] if n == 0 else wall.at[core, xd]
+        to = (z_peer(k), g) if n == 0 else (x_peer(k % 4), g if k < 4 else twin)
         return pltpu.make_async_remote_copy(
             ref, ref, pss.at[n, k], prs.at[n, k], device_id=to, device_id_type=MESH
         )
 
     def weights_from(n, k):
-        ref = [
-            wall.at[core, xd, lax.rem(zd + 4 - k, 4)],
-            wall.at[core, lax.rem(xd + 4 - k, 4)],
-            wall.at[1 - core],
-        ][n]
+        if n == 0:
+            ref = wall.at[core, xd, lax.rem(zd + 4 - k, 4)]
+        else:
+            ref = wall.at[core if k < 4 else 1 - core, lax.rem(xd + 8 - k, 4)]
         return pltpu.make_async_remote_copy(
             ref, ref, pss.at[n, k], prs.at[n, k], device_id=(d, twin), device_id_type=MESH
         )
 
     def weights_start(n):
-        for k in range(1, 4 if n < 2 else 2):
+        for k in range(1, 4 + 4 * n):
             weights_copy(n, k).start()
 
     def weights_wait(n):
-        for k in range(1, 4 if n < 2 else 2):
+        for k in range(1, 4 + 4 * n):
             weights_from(n, k).wait()
 
     def slab_copies(n, ts):
@@ -237,7 +237,7 @@
             src.at[t], dst.at[t], send.at[t], recv.at[t], device_id=(t, g), device_id_type=MESH
         )
 
-    pl.semaphore_wait(barrier, ND - 1 + 1 + 2 + 4)
+    pl.semaphore_wait(barrier, ND - 1 + 4 + 2 + 4)
     weights_start(0)
     for c in edge_copies(0):
         c.start()
@@ -321,8 +321,6 @@
     weights_wait(0)
     weights_start(1)
     complete(0, vs)
-    weights_wait(1)
-    weights_start(2)
 
     def first(i, edge):
         z = 2 * i
@@ -341,22 +339,18 @@
 
     half = iota((C, LANES), 1) < C
 
-    def diagonal(p):
-        def step(owner, _):
-            i = 2 * owner + p
-            w = wall[p, owner // 4, lax.rem(owner, 4)].astype(F32)
-            turned = pltpu.roll(w, C, 1)
-            top = [jnp.where(half, w, 0.0), jnp.where(half, turned, 0.0)]
-            bottom = [jnp.where(half, 0.0, turned), jnp.where(half, 0.0, w)]
-            bd[i, 0:C, :] = jnp.concatenate(top, axis=1).astype(BF16)
-            bd[i, C : 2 * C, :] = jnp.concatenate(bottom, axis=1).astype(BF16)
-            return 0
-
-        return step
-
-    lax.fori_loop(0, ND, diagonal(core), 0, unroll=4)
-    weights_wait(2)
-    lax.fori_loop(0, ND, diagonal(1 - core), 0, unroll=4)
+    def diagonal(i, _):
+        owner = i // 2
+        w = wall[lax.rem(i, 2), owner // 4, lax.rem(owner, 4)].astype(F32)
+        turned = pltpu.roll(w, C, 1)
+        top = [jnp.where(half, w, 0.0), jnp.where(half, turned, 0.0)]
+        bottom = [jnp.where(half, 0.0, turned), jnp.where(half, 0.0, w)]
+        bd[i, 0:C, :] = jnp.concatenate(top, axis=1).astype(BF16)
+        bd[i, C : 2 * C, :] = jnp.concatenate(bottom, axis=1).astype(BF16)
+        return 0
+
+    weights_wait(1)
+    lax.fori_loop(0, M // 2, diagonal, 0, unroll=4)
 
     loads[3].wait()
     loads[5].wait()
@@ -478,8 +472,8 @@
             dma((ND,)),
             dma((ND,)),
             dma((ND,)),
-            dma((3, 4)),
-            dma((3, 4)),
+            dma((2, 8)),
+            dma((2, 8)),
             dma((2, 8)),
             dma((2, 8)),
             dma((8,)),

time: 40.5 us -> 39.8 us (0.983)
  Pallas kernels: 37.8 us -> 37.2 us
    pallas_call x1, Pallas kernels: 37.8 us -> 37.2 us  [local(): pl.pallas_call(kernel, out_shape=jax.ShapeDtypeStruct((CD, ROWS, LANES),...]
where the time goes in v3:
time: 39.8 us; the launch traced here: 39.7 us
  Pallas kernels  37.2 us (93%)
  local copies, waits for them, and re-layouts  2.55 us (6%)
    pallas_call x1, Pallas kernels, local(): pl.pallas_call(kernel, out_shape=jax.ShapeDtypeStruct((CD, ROWS, LANES),...  37.2 us
    reshape x1, local copies, waits for them, and re-layouts, local(): return res.reshape(CD, C, 2, LANES).transpose(1, 0, 2, 3)  2.55 us

profile of v3, /device:TPU:1, one launch (start us, length us, event | category | flops | bytes accessed | tf_op | source)
XLA Modules:
  0.0 39.7 jit_solution(13705119777619963439)
XLA Ops:
  0.0 37.2 %shard_map.82 = bf16[24,128,128]{2,1,0:T(8,128)(2,1)} custom-call(bf16[64,24,2,128]{3,2,1,0:T(2,128)(2,1)} %vol_h.1, bf16[3,3,3,64,64]{4,3,2,1,0:T(8,128)(2,1)} %w1_h.1, bf16[3,3,3,64,64]{4,3,2,1,0:T(8,128)(2,1)} %w2_h.1, bf16[4,64,64]{2,1,0:T(8,128)(2,1)} %mw_h.1, bf16[160,384]{1,0:T(8,128)(2,1)} %constant.8.clone.hk_h, ...), custom_call_target="tpu_custom_call" | custom-call | tf_op jit(solution)/shard_map/pallas_call | solution.py:438
  37.2 2.6 %copy.11 = bf16[24,64,2,128]{3,2,0,1:T(2,128)(2,1)} copy(bf16[24,64,2,128]{3,2,1,0:T(2,128)(2,1)} %bitcast.4) | data formatting | bytes 1572864 | tf_op jit(solution)/shard_map/reshape | solution.py:485

commit v4 on v3

--- a/solution.py
+++ b/solution.py
@@ -349,19 +349,19 @@
         bd[i, C : 2 * C, :] = jnp.concatenate(bottom, axis=1).astype(BF16)
         return 0
 
+
+    loads[3].wait()
+    loads[5].wait()
+
+    def wait_forward(k, _):
+        spectral_from(fs, fr, fss, frs, depth_peer(k)).wait()
+        return 0
+
+    lax.fori_loop(1, ND, wait_forward, 0)
+    coef[...] = dot(gk[...], fr[...].reshape(ND * R * XO, LANES)).astype(BF16)
+
     weights_wait(1)
     lax.fori_loop(0, M // 2, diagonal, 0, unroll=4)
-
-    loads[3].wait()
-    loads[5].wait()
-
-    def wait_forward(k, _):
-        spectral_from(fs, fr, fss, frs, depth_peer(k)).wait()
-        return 0
-
-    lax.fori_loop(1, ND, wait_forward, 0)
-    coef[...] = dot(gk[...], fr[...].reshape(ND * R * XO, LANES)).astype(BF16)
-
     def mix(i, _):
         rows = pl.ds(pl.multiple_of(16 * i, 16), 16)
         res = dot(coef[rows, :], bd[i])

time: 39.8 us -> 38.4 us (0.965)
  Pallas kernels: 37.2 us -> 35.6 us
    pallas_call x1, Pallas kernels: 37.2 us -> 35.6 us  [local(): pl.pallas_call(kernel, out_shape=jax.ShapeDtypeStruct((CD, ROWS, LANES),...]
where the time goes in v4:
time: 38.4 us; the launch traced here: 38.1 us
  Pallas kernels  35.6 us (93%)
  local copies, waits for them, and re-layouts  2.55 us (7%)
    pallas_call x1, Pallas kernels, local(): pl.pallas_call(kernel, out_shape=jax.ShapeDtypeStruct((CD, ROWS, LANES),...  35.6 us
    reshape x1, local copies, waits for them, and re-layouts, local(): return res.reshape(CD, C, 2, LANES).transpose(1, 0, 2, 3)  2.55 us

profile of v4, /device:TPU:1, one launch (start us, length us, event | category | flops | bytes accessed | tf_op | source)
XLA Modules:
  0.0 38.1 jit_solution(15515091715288220786)
XLA Ops:
  0.0 35.6 %shard_map.82 = bf16[24,128,128]{2,1,0:T(8,128)(2,1)} custom-call(bf16[64,24,2,128]{3,2,1,0:T(2,128)(2,1)} %vol_h.1, bf16[3,3,3,64,64]{4,3,2,1,0:T(8,128)(2,1)} %w1_h.1, bf16[3,3,3,64,64]{4,3,2,1,0:T(8,128)(2,1)} %w2_h.1, bf16[4,64,64]{2,1,0:T(8,128)(2,1)} %mw_h.1, bf16[160,384]{1,0:T(8,128)(2,1)} %constant.8.clone.hk_h, ...), custom_call_target="tpu_custom_call" | custom-call | tf_op jit(solution)/shard_map/pallas_call | solution.py:438
  35.6 2.6 %copy.11 = bf16[24,64,2,128]{3,2,0,1:T(2,128)(2,1)} copy(bf16[24,64,2,128]{3,2,1,0:T(2,128)(2,1)} %bitcast.4) | data formatting | bytes 1572864 | tf_op jit(solution)/shard_map/reshape | solution.py:485
